TPU v7x, 32 devices: a whole 2x2x4 slice. The times are simulated.
32 devices in a mesh: span: 8 (over z, x), sp: 2 (over y), fsdp: 2 (over core).
Axes of the slice: x: 2, y: 2, z: 4, core: 2. Of those that a mesh axis runs over, the one named last changes fastest.
Arguments:
- query_pre: bfloat16 [2, 2048, 3072], P('fsdp', ('span', 'sp')), may hold values from -12 to 12
- key_pre: bfloat16 [2, 2048, 3072], P('fsdp', ('span', 'sp')), may hold values from -12 to 12
- values: bfloat16 [2, 2048, 3072], P('fsdp', ('span', 'sp')), may hold values from -6 to 6
- cotangent: bfloat16 [2, 2048, 3072], P('fsdp', ('span', 'sp')), may hold values from -6 to 6
- gains: float32 [2, 3072], P(None, 'fsdp'), may hold values from 0.5 to 1.5
- frame_span: int32 [2, 2048], P('fsdp', 'span'), may hold values from 0 to 15, as said below
- denoise_steps: int32 [2, 16], P('fsdp'), may hold values from 1 to 4
Outputs:
- query_grad: bfloat16 [2, 2048, 3072], P('fsdp', ('span', 'sp'))
- key_grad: bfloat16 [2, 2048, 3072], P('fsdp', ('span', 'sp'))
- value_grad: bfloat16 [2, 2048, 3072], P('fsdp', ('span', 'sp'))
- gain_grad: float32 [2, 3072], P(None, 'fsdp')
Inputs may be any that keep to these rules, and one draw needn't show every extreme that they name: `frame_span`: never falls along a video. Group g (tokens g * 256 to (g + 1) * 256 - 1) holds frame spans 2 g and 2 g + 1, each from a quarter to three quarters of the group's tokens.
All inputs are finite; a program needn't handle non-finite values.
Results may differ from a plain program's by a relative error of at most 0.0081.
The roundings to bfloat16 on the way count: a program that leaves them out, or rounds other values in their place, can miss the bound.
Values may be sent and summed in bfloat16 or wider, within the bound.
A program may use at most 128 MiB of HBM per device.

v0:
```python
import jax
import jax.numpy as jnp
from jax import lax
from jax.sharding import PartitionSpec as P

HDIM = 128


EPSILON = 1e-06
NEGATIVE = -1e30


def from_behind(value, axis, steps):
    count = lax.axis_size(axis)
    first, last = (max(0, -steps), min(count, count - steps))
    return lax.ppermute(value, axis, [(source, source + steps) for source in range(first, last)])


def normed(raw_rows, gain_row):
    wide = raw_rows.astype(jnp.float32)
    inverse_rms = lax.rsqrt(jnp.mean(wide * wide, axis=-1, keepdims=True) + EPSILON)
    normal_rows = wide * inverse_rms
    return (normal_rows, inverse_rms, (normal_rows * gain_row).astype(jnp.bfloat16))


def norm_backward(grad_rows, normal_rows, inverse_rms, gain_row):
    upstream = grad_rows.astype(jnp.float32)
    scaled = upstream * gain_row
    inner = jnp.mean(scaled * normal_rows, axis=-1, keepdims=True)
    result = (inverse_rms * (scaled - normal_rows * inner)).astype(jnp.bfloat16)
    return (result, jnp.sum(upstream * normal_rows, axis=0))


def across(left, right):
    return lax.dot_general(
        left, right, (((1,), (1,)), ((), ())), preferred_element_type=jnp.float32
    )


def downward(left, right):
    return lax.dot_general(
        left, right, (((0,), (0,)), ((), ())), preferred_element_type=jnp.float32
    )


def head_grads(
    query_head, grad_head, key_joined, value_joined, joined_mask, step_weight, own_width
):
    score_scale = HDIM ** (-0.5)
    scores = across(query_head, key_joined) * score_scale
    masked = jnp.where(joined_mask, scores, NEGATIVE)
    row_max = jnp.max(masked, axis=1)
    row_total = jnp.sum(jnp.exp(masked - row_max[:, None]), axis=1)
    log_total = row_max + jnp.log(row_total)
    grad_prob = across(grad_head, value_joined)
    probs = jnp.where(joined_mask, jnp.exp(scores - log_total[:, None]), 0.0)
    row_delta = jnp.sum(probs * grad_prob, axis=1)
    factor = step_weight[:, None]
    sgrad = (factor * probs * (grad_prob - row_delta[:, None])).astype(jnp.bfloat16)
    weights = (factor * probs).astype(jnp.bfloat16)
    query_part = jnp.dot(sgrad, key_joined, preferred_element_type=jnp.float32) * score_scale
    key_own_grad = downward(sgrad[:, :own_width], query_head) * score_scale
    value_own_grad = downward(weights[:, :own_width], grad_head)
    return (
        query_part,
        key_own_grad,
        value_own_grad,
        sgrad[:, own_width:],
        weights[:, own_width:],
        log_total,
        row_delta,
    )


def on_device(query_pre, key_pre, values, cotangent, gains, frame_span, denoise_steps):
    gain_full = lax.all_gather(gains, "fsdp", axis=1, tiled=True)
    q_normal, q_inverse, q_ready = normed(query_pre[0], gain_full[0])
    k_normal, k_inverse, k_ready = normed(key_pre[0], gain_full[1])
    heads_query, heads_key, heads_value, heads_grad = (
        lax.all_to_all(q_ready, "sp", split_axis=1, concat_axis=0, tiled=True),
        lax.all_to_all(k_ready, "sp", split_axis=1, concat_axis=0, tiled=True),
        lax.all_to_all(values[0], "sp", split_axis=1, concat_axis=0, tiled=True),
        lax.all_to_all(cotangent[0], "sp", split_axis=1, concat_axis=0, tiled=True),
    )
    head_count = heads_query.shape[1] // HDIM
    own_width = heads_query.shape[0]
    span_ids = frame_span[0]
    step_table = denoise_steps[0].astype(jnp.float32)
    matches = span_ids[:, None] == lax.iota(jnp.int32, step_table.shape[0])[None, :]
    step_weight = jnp.sum(jnp.where(matches, step_table[None, :], 0.0), axis=1)
    group_index = lax.axis_index("span")
    key_prev, value_prev = from_behind((heads_key, heads_value), "span", 1)
    own_mask = span_ids[None, :] <= span_ids[:, None]
    prev_open = group_index > 0
    prev_mask = jnp.broadcast_to(prev_open, own_mask.shape)
    joined_mask = jnp.concatenate([own_mask, prev_mask], axis=1)
    key_joined_all = jnp.concatenate([heads_key, key_prev], axis=0)
    value_joined_all = jnp.concatenate([heads_value, value_prev], axis=0)
    query_parts = []
    key_parts = []
    value_parts = []
    sgrad_list = []
    weight_list = []
    total_list = []
    delta_list = []
    for head_index in range(head_count):
        first = head_index * HDIM
        last = first + HDIM
        outcome = head_grads(
            heads_query[:, first:last],
            heads_grad[:, first:last],
            key_joined_all[:, first:last],
            value_joined_all[:, first:last],
            joined_mask,
            step_weight,
            own_width,
        )
        query_parts.append(outcome[0])
        key_parts.append(outcome[1])
        value_parts.append(outcome[2])
        sgrad_list.append(outcome[3])
        weight_list.append(outcome[4])
        total_list.append(outcome[5])
        delta_list.append(outcome[6])
    query_attn = jnp.concatenate(query_parts, axis=1)
    key_own = jnp.concatenate(key_parts, axis=1)
    value_own = jnp.concatenate(value_parts, axis=1)
    key_terms = []
    value_terms = []
    for head_index in range(head_count):
        first = head_index * HDIM
        last = first + HDIM
        key_terms.append(
            downward(sgrad_list[head_index], heads_query[:, first:last]) * HDIM ** (-0.5)
        )
        value_terms.append(downward(weight_list[head_index], heads_grad[:, first:last]))
    key_back, value_back = from_behind(
        (jnp.concatenate(key_terms, axis=1), jnp.concatenate(value_terms, axis=1)), "span", -1
    )
    key_attn = key_own + key_back
    value_attn = value_own + value_back
    query_tokens, key_tokens, value_tokens = (
        lax.all_to_all(
            query_attn.astype(jnp.bfloat16), "sp", split_axis=0, concat_axis=1, tiled=True
        ),
        lax.all_to_all(
            key_attn.astype(jnp.bfloat16), "sp", split_axis=0, concat_axis=1, tiled=True
        ),
        lax.all_to_all(
            value_attn.astype(jnp.bfloat16), "sp", split_axis=0, concat_axis=1, tiled=True
        ),
    )
    query_back, query_gain = norm_backward(query_tokens, q_normal, q_inverse, gain_full[0])
    key_back_rows, key_gain = norm_backward(key_tokens, k_normal, k_inverse, gain_full[1])
    partial_value = jnp.stack([query_gain, key_gain])
    summed = lax.psum(partial_value, ("span", "sp"))
    gain_grad = lax.psum_scatter(summed, "fsdp", scatter_dimension=1, tiled=True)
    return (query_back[None], key_back_rows[None], value_tokens[None], gain_grad)


def solution(mesh):
    placed = (
        P("fsdp", ("span", "sp"), None),
        P("fsdp", ("span", "sp"), None),
        P("fsdp", ("span", "sp"), None),
        P("fsdp", ("span", "sp"), None),
        P(None, "fsdp"),
        P("fsdp", "span"),
        P("fsdp", None),
    )
    return jax.shard_map(
        on_device,
        mesh=mesh,
        in_specs=placed,
        out_specs=(
            P("fsdp", ("span", "sp"), None),
            P("fsdp", ("span", "sp"), None),
            P("fsdp", ("span", "sp"), None),
            P(None, "fsdp"),
        ),
        check_vma=False,
    )
```

profile of v0, /device:TPU:0, one launch (start us, length us, event | category | flops | bytes accessed | tf_op | source)
XLA Modules:
  0.0 337.7 jit_solution(11438805276481410407)
XLA Ops:
  7.2 2.6 reshape.367
  13.4 4.1 %all-to-all-start.1 = ((bf16[128,2,1536]{2,0,1:T(8,128)(2,1)}), bf16[128,2,1536]{2,0,1:T(8,128)(2,1)S(1)}, u32[]{:S(2)}, u32[]{:S(2)}) async-start(bf16[128,2,1536]{2,0,1:T(8,128)(2,1)} %multiply_convert_fusion.2), calls=%async_computation.1 | async-start | bytes 1572864 | tf_op jit(solution)/shard_map/all_to_all | solution.py:81
  18.7 10.8 %all-to-all-done.1 = bf16[128,2,1536]{2,0,1:T(8,128)(2,1)S(1)} async-done(((bf16[128,2,1536]{2,0,1:T(8,128)(2,1)}), bf16[128,2,1536]{2,0,1:T(8,128)(2,1)S(1)}, u32[]{:S(2)}, u32[]{:S(2)}) %all-to-all-start.1) | async-done | bytes 786464 | tf_op jit(solution)/shard_map/all_to_all | solution.py:81
  29.5 4.3 %all-to-all-start.2 = ((bf16[128,2,1536]{0,2,1:T(8,128)(2,1)}), bf16[128,2,1536]{0,2,1:T(8,128)(2,1)}, u32[]{:S(2)}, u32[]{:S(2)}) async-start(bf16[128,2,1536]{0,2,1:T(8,128)(2,1)} %bitcast.7), calls=%async_computation.2 | async-start | bytes 1572864 | tf_op jit(solution)/shard_map/all_to_all | solution.py:82
  35.4 2.8 copy.188
  38.5 3.7 %collective-permute-start = (bf16[256,1536]{1,0:T(8,128)(2,1)S(1)}, bf16[256,1536]{1,0:T(8,128)(2,1)S(1)}, u32[]{:S(2)}, u32[]{:S(2)}) collective-permute-start(bf16[256,1536]{1,0:T(8,128)(2,1)S(1)} %bitcast.96), channel_id=1, source_target_pairs={{0,4},{4,8},{8,12},{12,16},{16,20},{20,24},{24,28},{1,5},{5,9},{9,... | collective-permute-start | bytes 2359304 | tf_op jit(solution)/shard_map/ppermute | solution.py:16
  42.1 2.6 all-to-all-done.2
  44.8 4.3 %all-to-all-start.3 = ((bf16[128,2,1536]{0,2,1:T(8,128)(2,1)}), bf16[128,2,1536]{0,2,1:T(8,128)(2,1)}, u32[]{:S(2)}, u32[]{:S(2)}) async-start(bf16[128,2,1536]{0,2,1:T(8,128)(2,1)} %bitcast.170), calls=%async_computation.3 | async-start | bytes 1572864 | tf_op jit(solution)/shard_map/all_to_all | solution.py:83
  50.4 8.8 %all-to-all-done.3 = bf16[128,2,1536]{0,2,1:T(8,128)(2,1)} async-done(((bf16[128,2,1536]{0,2,1:T(8,128)(2,1)}), bf16[128,2,1536]{0,2,1:T(8,128)(2,1)}, u32[]{:S(2)}, u32[]{:S(2)}) %all-to-all-start.3) | async-done | bytes 786464 | tf_op jit(solution)/shard_map/all_to_all | solution.py:83
  59.2 4.3 %all-to-all-start = ((bf16[128,2,1536]{2,0,1:T(8,128)(2,1)}), bf16[128,2,1536]{2,0,1:T(8,128)(2,1)}, u32[]{:S(2)}, u32[]{:S(2)}) async-start(bf16[128,2,1536]{2,0,1:T(8,128)(2,1)} %multiply_convert_fusion.3), calls=%async_computation | async-start | bytes 1572864 | tf_op jit(solution)/shard_map/all_to_all | solution.py:80
  65.2 3.2 collective-permute-start.1
  114.6 3.9 %all-to-all-start.4 = ((bf16[2,128,1536]{2,1,0:T(8,128)(2,1)}), bf16[2,128,1536]{2,1,0:T(8,128)(2,1)S(1)}, u32[]{:S(2)}, u32[]{:S(2)}) async-start(bf16[2,128,1536]{2,1,0:T(8,128)(2,1)} %constant_dynamic-update-slice_fusion), calls=%async_computation.4 | async-start | bytes 1572864 | tf_op jit(solution)/shard_map/all_to_all | solution.py:143
  180.4 2.4 copy.202
  182.8 2.7 reshape.368
  186.8 10.2 %collective-permute-done.2 = f32[256,1536]{1,0:T(8,128)} collective-permute-done((f32[256,1536]{1,0:T(8,128)}, f32[256,1536]{1,0:T(8,128)}, u32[]{:S(2)}, u32[]{:S(2)}) %collective-permute-start.2) | collective-permute-done | bytes 1572896 | tf_op jit(solution)/shard_map/ppermute | solution.py:16
  197.1 2.5 add_convert_fusion.1
  199.6 3.5 %all-to-all-start.5 = ((bf16[2,128,1536]{2,1,0:T(8,128)(2,1)}), bf16[2,128,1536]{2,1,0:T(8,128)(2,1)S(1)}, u32[]{:S(2)}, u32[]{:S(2)}) async-start(bf16[2,128,1536]{2,1,0:T(8,128)(2,1)} %bitcast.40), calls=%async_computation.5 | async-start | bytes 1572864 | tf_op jit(solution)/shard_map/all_to_all | solution.py:146
  203.1 23.6 %collective-permute-done.3 = f32[256,1536]{0,1:T(8,128)} collective-permute-done((f32[256,1536]{0,1:T(8,128)}, f32[256,1536]{0,1:T(8,128)}, u32[]{:S(2)}, u32[]{:S(2)}) %collective-permute-start.3) | collective-permute-done | bytes 1572896 | tf_op jit(solution)/shard_map/ppermute | solution.py:16
  226.7 2.9 copy_bitcast_fusion
  229.6 4.3 %all-to-all-start.6 = ((bf16[2,128,1536]{1,2,0:T(8,128)(2,1)}), bf16[2,128,1536]{1,2,0:T(8,128)(2,1)}, u32[]{:S(2)}, u32[]{:S(2)}) async-start(bf16[2,128,1536]{1,2,0:T(8,128)(2,1)} %copy_bitcast_fusion), calls=%async_computation.6 | async-start | bytes 1572864 | tf_op jit(solution)/shard_map/all_to_all | solution.py:149
  234.4 2.4 copy.227
  236.8 3.5 %reshape.369 = f32[1,128,3072]{2,1,0:T(8,128)} reshape(f32[128,2,1536]{2,1,0:T(2,128)} %copy.227) | data formatting | bytes 3145728 | tf_op jit(solution)/shard_map/convert_element_type | solution.py:27
  246.8 5.6 %reduce-scatter.4.cloned.1.call-done = f32[1536,2]{1,0:T(8,128)} async-done(((f32[3072,2]{1,0:T(8,128)}), f32[1536,2]{1,0:T(8,128)}) %reduce-scatter.4.cloned.1.call-update) | async-done | bytes 12304
  253.8 77.0 %psum.8 = f32[2,1536]{1,0:T(2,128)} all-reduce(f32[2,1536]{1,0:T(2,128)S(1)} %copy.267), channel_id=1, replica_groups=mesh['span'=8,'sp'=2,'fsdp'=2] {'span','sp'}, use_global_device_ids=true, to_apply=%region_43.44 | all-reduce | flops 3072 | bytes 24576 | tf_op jit(solution)/shard_map/psum | solution.py:156
  (252 shorter events, 126.7 us)
Async XLA Ops:
  13.4 16.0 %all-to-all-start.1 = ((bf16[128,2,1536]{2,0,1:T(8,128)(2,1)}), bf16[128,2,1536]{2,0,1:T(8,128)(2,1)S(1)}, u32[]{:S(2)}, u32[]{:S(2)}) async-start(bf16[128,2,1536]{2,0,1:T(8,128)(2,1)} %multiply_convert_fusion.2), calls=%async_computation.1 | async-start | bytes 1572864 | tf_op jit(solution)/shard_map/all_to_all | solution.py:81
  17.5 16.2 %copy-start.6 = (bf16[1,128,3072]{2,1,0:T(8,128)(2,1)S(1)}, bf16[1,128,3072]{2,1,0:T(8,128)(2,1)}, u32[]{:S(2)}) copy-start(bf16[1,128,3072]{2,1,0:T(8,128)(2,1)} %param.7) | copy-start | bytes 2359300
  29.5 15.3 %all-to-all-start.2 = ((bf16[128,2,1536]{0,2,1:T(8,128)(2,1)}), bf16[128,2,1536]{0,2,1:T(8,128)(2,1)}, u32[]{:S(2)}, u32[]{:S(2)}) async-start(bf16[128,2,1536]{0,2,1:T(8,128)(2,1)} %bitcast.7), calls=%async_computation.2 | async-start | bytes 1572864 | tf_op jit(solution)/shard_map/all_to_all | solution.py:82
  38.5 34.2 %collective-permute-start = (bf16[256,1536]{1,0:T(8,128)(2,1)S(1)}, bf16[256,1536]{1,0:T(8,128)(2,1)S(1)}, u32[]{:S(2)}, u32[]{:S(2)}) collective-permute-start(bf16[256,1536]{1,0:T(8,128)(2,1)S(1)} %bitcast.96), channel_id=1, source_target_pairs={{0,4},{4,8},{8,12},{12,16},{16,20},{20,24},{24,28},{1,5},{5,9},{9,... | collective-permute-start | bytes 2359304 | tf_op jit(solution)/shard_map/ppermute | solution.py:16
  44.8 14.4 %all-to-all-start.3 = ((bf16[128,2,1536]{0,2,1:T(8,128)(2,1)}), bf16[128,2,1536]{0,2,1:T(8,128)(2,1)}, u32[]{:S(2)}, u32[]{:S(2)}) async-start(bf16[128,2,1536]{0,2,1:T(8,128)(2,1)} %bitcast.170), calls=%async_computation.3 | async-start | bytes 1572864 | tf_op jit(solution)/shard_map/all_to_all | solution.py:83
  49.1 14.4 %copy-start.48 = (s32[1,256]{1,0:T(1,128)S(1)}, s32[1,256]{1,0:T(1,128)}, u32[]{:S(2)}) copy-start(s32[1,256]{1,0:T(1,128)} %param.12) | copy-start | bytes 3076
  59.2 13.5 %all-to-all-start = ((bf16[128,2,1536]{2,0,1:T(8,128)(2,1)}), bf16[128,2,1536]{2,0,1:T(8,128)(2,1)}, u32[]{:S(2)}, u32[]{:S(2)}) async-start(bf16[128,2,1536]{2,0,1:T(8,128)(2,1)} %multiply_convert_fusion.3), calls=%async_computation | async-start | bytes 1572864 | tf_op jit(solution)/shard_map/all_to_all | solution.py:80
  65.2 19.1 %collective-permute-start.1 = (bf16[256,1536]{1,0:T(8,128)(2,1)S(1)}, bf16[256,1536]{1,0:T(8,128)(2,1)S(1)}, u32[]{:S(2)}, u32[]{:S(2)}) collective-permute-start(bf16[256,1536]{1,0:T(8,128)(2,1)S(1)} %bitcast.120), channel_id=1, source_target_pairs={{0,4},{4,8},{8,12},{12,16},{16,20},{20,24},{24,28},{1,5},{5,9},{9,... | collective-permute-start | bytes 2359304 | tf_op jit(solution)/shard_map/ppermute | solution.py:16
  114.6 14.5 %copy-start.24 = (bf16[256,512]{1,0:T(8,128)(2,1)S(1)}, bf16[256,512]{1,0:T(8,128)(2,1)}, u32[]{:S(2)}) copy-start(bf16[256,512]{1,0:T(8,128)(2,1)} %copy-done.23) | copy-start | bytes 786436
  114.6 16.3 %copy-start.32 = (bf16[256,512]{1,0:T(8,128)(2,1)S(1)}, bf16[256,512]{1,0:T(8,128)(2,1)}, u32[]{:S(2)}) copy-start(bf16[256,512]{1,0:T(8,128)(2,1)} %copy-done.31) | copy-start | bytes 786436
  114.6 64.9 %all-to-all-start.4 = ((bf16[2,128,1536]{2,1,0:T(8,128)(2,1)}), bf16[2,128,1536]{2,1,0:T(8,128)(2,1)S(1)}, u32[]{:S(2)}, u32[]{:S(2)}) async-start(bf16[2,128,1536]{2,1,0:T(8,128)(2,1)} %constant_dynamic-update-slice_fusion), calls=%async_computation.4 | async-start | bytes 1572864 | tf_op jit(solution)/shard_map/all_to_all | solution.py:143
  118.5 16.0 %copy-start.14 = (bf16[256,512]{1,0:T(8,128)(2,1)S(1)}, bf16[256,512]{1,0:T(8,128)(2,1)}, u32[]{:S(2)}) copy-start(bf16[256,512]{1,0:T(8,128)(2,1)} %copy-done.13) | copy-start | bytes 786436
  129.0 17.8 %copy-start.28 = (bf16[256,512]{1,0:T(8,128)(2,1)S(1)}, bf16[256,512]{1,0:T(8,128)(2,1)}, u32[]{:S(2)}) copy-start(bf16[256,512]{1,0:T(8,128)(2,1)} %copy-done.26) | copy-start | bytes 786436
  130.8 17.8 %copy-start.25 = (bf16[256,512]{1,0:T(8,128)(2,1)S(1)}, bf16[256,512]{1,0:T(8,128)(2,1)}, u32[]{:S(2)}) copy-start(bf16[256,512]{1,0:T(8,128)(2,1)} %copy-done.23) | copy-start | bytes 786436
  132.6 17.8 %copy-start.33 = (bf16[256,512]{1,0:T(8,128)(2,1)S(1)}, bf16[256,512]{1,0:T(8,128)(2,1)}, u32[]{:S(2)}) copy-start(bf16[256,512]{1,0:T(8,128)(2,1)} %copy-done.31) | copy-start | bytes 786436
  139.7 19.2 %copy-start.5 = (bf16[2,128,1536]{2,1,0:T(8,128)(2,1)S(1)}, bf16[2,128,1536]{2,1,0:T(8,128)(2,1)}, u32[]{:S(2)}) copy-start(bf16[2,128,1536]{2,1,0:T(8,128)(2,1)} %copy.189) | copy-start | bytes 2359300
  139.7 19.2 %copy-start.35 = (bf16[256,512]{1,0:T(8,128)(2,1)S(1)}, bf16[256,512]{1,0:T(8,128)(2,1)}, u32[]{:S(2)}) copy-start(bf16[256,512]{1,0:T(8,128)(2,1)} %get-tuple-element.73) | copy-start | bytes 786436
  143.3 17.3 %copy-start.39 = (bf16[256,512]{1,0:T(8,128)(2,1)S(1)}, bf16[256,512]{1,0:T(8,128)(2,1)}, u32[]{:S(2)}) copy-start(bf16[256,512]{1,0:T(8,128)(2,1)} %get-tuple-element.86) | copy-start | bytes 786436
  146.8 15.5 %copy-start.38 = (bf16[256,512]{1,0:T(8,128)(2,1)S(1)}, bf16[256,512]{1,0:T(8,128)(2,1)}, u32[]{:S(2)}) copy-start(bf16[256,512]{1,0:T(8,128)(2,1)} %get-tuple-element.69) | copy-start | bytes 786436
  157.5 39.5 %collective-permute-start.2 = (f32[256,1536]{1,0:T(8,128)}, f32[256,1536]{1,0:T(8,128)}, u32[]{:S(2)}, u32[]{:S(2)}) collective-permute-start(f32[256,1536]{1,0:T(8,128)} %fusion), channel_id=1, source_target_pairs={{4,0},{8,4},{12,8},{16,12},{20,16},{24,20},{28,24},{5,1},{9,5},{13... | collective-permute-start | bytes 4718600 | tf_op jit(solution)/shard_map/ppermute | solution.py:16
  176.3 50.4 %collective-permute-start.3 = (f32[256,1536]{0,1:T(8,128)}, f32[256,1536]{0,1:T(8,128)}, u32[]{:S(2)}, u32[]{:S(2)}) collective-permute-start(f32[256,1536]{0,1:T(8,128)} %convolution_dynamic-update-slice_fusion), channel_id=1, source_target_pairs={{4,0},{8,4},{12,8},{16,12},{20,16},{24,20},{28,24},{5,1},{9,5},{13... | collective-permute-start | bytes 4718600 | tf_op jit(solution)/shard_map/ppermute | solution.py:16
  199.6 30.0 %all-to-all-start.5 = ((bf16[2,128,1536]{2,1,0:T(8,128)(2,1)}), bf16[2,128,1536]{2,1,0:T(8,128)(2,1)S(1)}, u32[]{:S(2)}, u32[]{:S(2)}) async-start(bf16[2,128,1536]{2,1,0:T(8,128)(2,1)} %bitcast.40), calls=%async_computation.5 | async-start | bytes 1572864 | tf_op jit(solution)/shard_map/all_to_all | solution.py:146
  229.6 14.9 %all-to-all-start.6 = ((bf16[2,128,1536]{1,2,0:T(8,128)(2,1)}), bf16[2,128,1536]{1,2,0:T(8,128)(2,1)}, u32[]{:S(2)}, u32[]{:S(2)}) async-start(bf16[2,128,1536]{1,2,0:T(8,128)(2,1)} %copy_bitcast_fusion), calls=%async_computation.6 | async-start | bytes 1572864 | tf_op jit(solution)/shard_map/all_to_all | solution.py:149
  233.9 18.5 %reduce-scatter.4.cloned.1.call-start = ((), (), s32[]{:S(2)}) async-start(), calls=%async_computation.8 | async-start | bytes 2359296
  (38 other events, 252.4 us)
Sparse Core Ops, SparseCore 0:
  243.0 9.3 reduce-scatter.3
where the time goes:
time: 340 us; the launch traced here: 338 us
  matrix products  84.9 us (25%)
  blocking collectives  79 us (23%)
  waiting for transfers between devices  63.7 us (19%)
  starting transfers between devices  38.6 us (11%)
  local copies, waits for them, and re-layouts  36.5 us (11%)
  other arithmetic  20.2 us (6%)
  between operations  14.8 us (4%)
    psum x1, blocking collectives, on_device(): summed = lax.psum(partial_value, ('span', 'sp'))  77 us
    dot_general x48, matrix products, downward(): lax.dot_general(left, right, (((0,), (0,)), ((), ())), preferred_element_...  63.4 us
    ppermute x4, waiting for transfers between devices, from_behind(): lax.ppermute(value, axis, [(source, source + steps) for source in range(f...  33.8 us
    dot_general x24, matrix products, across(): lax.dot_general(left, right, (((1,), (1,)), ((), ())), preferred_element_...  18.8 us
    unnamed x118, local copies, waits for them, and re-layouts  16.9 us
    convert_element_type x4, local copies, waits for them, and re-layouts, norm_backward(): upstream = grad_rows.astype(jnp.float32)  11 us
    all_to_all x1, waiting for transfers between devices, on_device(): lax.all_to_all(k_ready, 'sp', split_axis=1, concat_axis=0, tiled=True)  10.8 us
    ppermute x4, starting transfers between devices, from_behind(): lax.ppermute(value, axis, [(source, source + steps) for source in range(f...  9.53 us
  transfers between devices with their start and end apart: 12, of which 7 were waited for; matrix products, arithmetic and copies ran while one was open for 31% of the time, Pallas kernels for 0%

commit v1 on v0

v1 whole, which is shorter than its diff:
```python
import functools
import math

import jax
import jax.numpy as jnp
from jax import lax
from jax.experimental import pallas as pl
from jax.experimental.pallas import tpu as pltpu
from jax.sharding import PartitionSpec as P

HDIM = 128
EPSILON = 1e-06
NEGATIVE = -1e30
F32 = jnp.float32
BF16 = jnp.bfloat16
ROWS = 16


def dot(left, right, left_dim, right_dim):
    return lax.dot_general(
        left, right, (((left_dim,), (right_dim,)), ((), ())), preferred_element_type=F32
    )


def kernel(
    sizes,
    query_ref, key_ref, value_ref, grad_ref, gain_ref, span_ref, steps_ref,
    query_out, key_out, value_out, gain_out,
    gain_full, q_ready, k_ready, q_inverse, k_inverse,
    heads_query, heads_grad, key_joined, value_joined, bias, weight_row,
    own_key, own_value, send_key, send_value, back_key, back_value,
    dq_heads, dk_heads, dv_heads, dq_rows, dk_rows, dv_rows,
    gain_part, gain_rows, pair_recv, tree_send, tree_recv,
    gain_s, gain_r, in_s, in_r, in_local, ahead_s, ahead_r, behind_s, behind_r,
    out_s, out_r, out_local, pair_s, pair_r, tree_s, tree_r,
):
    n_span, n_sp, n_fsdp, chunks, per_chunk = sizes
    tokens, channels = q_ready.shape
    group, width = heads_query.shape
    part = channels // n_fsdp
    chunk_width = per_chunk * HDIM
    query_block = math.gcd(group, 256)
    scale = HDIM ** (-0.5)
    g, s, f = lax.axis_index("span"), lax.axis_index("sp"), lax.axis_index("fsdp")
    after, before = lax.rem(g + 1, n_span), lax.rem(g + n_span - 1, n_span)
    has_before, has_after = g > 0, g < n_span - 1

    def partner(index, step):
        return index + step * (1 - 2 * lax.rem(index // step, 2))

    sp_steps = [1 << b for b in range(n_sp.bit_length() - 1)]
    span_steps = [1 << b for b in range(n_span.bit_length() - 1)]
    tree = [("sp", partner(s, step)) for step in sp_steps]
    tree += [("span", partner(g, step)) for step in span_steps]

    barrier = pltpu.get_barrier_semaphore()

    def greet(device):
        pl.semaphore_signal(
            barrier, inc=1, device_id=device, device_id_type=pl.DeviceIdType.MESH
        )

    count = 0
    for d in range(1, n_fsdp):
        greet({"fsdp": lax.rem(f + d, n_fsdp)})
        count += 1
    for d in range(1, n_sp):
        greet({"sp": lax.rem(s + d, n_sp)})
        count += 1
    for step in span_steps[1:]:
        greet({"span": partner(g, step)})
        count += 1

    @pl.when(has_before)
    def _():
        greet({"span": before})

    @pl.when(has_after)
    def _():
        greet({"span": after})

    count += lax.div(g + n_span - 1, n_span) + lax.div(2 * n_span - 2 - g, n_span)
    pl.semaphore_wait(barrier, count)

    def remote(src, dst, send, recv, device):
        return pltpu.make_async_remote_copy(
            src_ref=src, dst_ref=dst, send_sem=send, recv_sem=recv,
            device_id=device, device_id_type=pl.DeviceIdType.MESH,
        )

    def columns(c):
        return pl.ds(pl.multiple_of(c * chunk_width, HDIM), chunk_width)

    def shifted(base, c):
        return pl.ds(pl.multiple_of(base * width + c * chunk_width, HDIM), chunk_width)

    def row_block(index):
        return pl.ds(pl.multiple_of(index * tokens, tokens), tokens)

    sources = (k_ready, value_ref.at[0], q_ready, grad_ref.at[0])
    homes = (key_joined, value_joined, heads_query, heads_grad)

    def incoming(a, c, d):
        peer = lax.rem(s + d, n_sp)
        return remote(
            sources[a].at[:, shifted(peer, c)], homes[a].at[row_block(s), columns(c)],
            in_s.at[a, c, d - 1], in_r.at[a, c, d - 1], {"sp": peer},
        )

    def incoming_local(a):
        return pltpu.make_async_copy(
            sources[a].at[:, pl.ds(pl.multiple_of(s * width, HDIM), width)],
            homes[a].at[row_block(s), :], in_local.at[a],
        )

    def ahead(a, c):
        home = homes[a]
        return remote(
            home.at[pl.ds(0, group), columns(c)], home.at[pl.ds(group, group), columns(c)],
            ahead_s.at[a, c], ahead_r.at[a, c], {"span": after},
        )

    def behind(a, c):
        return remote(
            (send_key, send_value)[a].at[:, columns(c)],
            (back_key, back_value)[a].at[:, columns(c)],
            behind_s.at[a, c], behind_r.at[a, c], {"span": before},
        )

    results = (dq_heads, dk_heads, dv_heads)
    landed = (dq_rows, dk_rows, dv_rows)

    def outgoing(a, c, d):
        peer = lax.rem(s + d, n_sp)
        return remote(
            results[a].at[row_block(peer), columns(c)], landed[a].at[:, shifted(s, c)],
            out_s.at[a, c, d - 1], out_r.at[a, c, d - 1], {"sp": peer},
        )

    def outgoing_local(a, c):
        return pltpu.make_async_copy(
            results[a].at[row_block(s), columns(c)], landed[a].at[:, shifted(s, c)],
            out_local.at[a, c],
        )

    def gain_copy(d):
        mine = pl.ds(pl.multiple_of(f * part, HDIM), part)
        return remote(
            gain_ref, gain_full.at[:, mine], gain_s.at[d - 1], gain_r.at[d - 1],
            {"fsdp": lax.rem(f + d, n_fsdp)},
        )

    peers = range(1, n_sp)
    for d in range(1, n_fsdp):
        gain_copy(d).start()
    for a in (1, 3):
        for d in peers:
            incoming(a, 0, d).start()
        incoming_local(a).start()
    gain_full[:, pl.ds(pl.multiple_of(f * part, HDIM), part)] = gain_ref[...]

    @pl.when(g == 0)
    def _():
        key_joined[group:, :] = jnp.zeros((group, width), BF16)
        value_joined[group:, :] = jnp.zeros((group, width), BF16)

    @pl.when(g == n_span - 1)
    def _():
        back_key[...] = jnp.zeros_like(back_key)
        back_value[...] = jnp.zeros_like(back_value)

    for d in range(1, n_fsdp):
        gain_copy(d).wait_recv()

    def norm(raw_ref, row, inverse_ref, ready_ref):
        def block(i, carry):
            rows = pl.ds(pl.multiple_of(i * ROWS, ROWS), ROWS)
            wide = raw_ref[0, rows, :].astype(F32)
            inverse = lax.rsqrt(
                jnp.sum(wide * wide, axis=1, keepdims=True) * (1.0 / channels) + EPSILON
            )
            inverse_ref[rows, :] = inverse
            ready_ref[rows, :] = (wide * inverse * gain_full[row : row + 1, :]).astype(BF16)
            return carry

        lax.fori_loop(0, tokens // ROWS, block, 0)

    norm(key_ref, 1, k_inverse, k_ready)
    for d in peers:
        incoming(0, 0, d).start()
    incoming_local(0).start()
    norm(query_ref, 0, q_inverse, q_ready)
    for d in peers:
        incoming(2, 0, d).start()
    incoming_local(2).start()

    def start_chunk(c, carry):
        for a in range(4):
            for d in peers:
                incoming(a, c, d).start()
        return carry

    lax.fori_loop(1, chunks, start_chunk, 0)

    ids = span_ref[...]
    ids_down = jnp.transpose(jnp.broadcast_to(ids.astype(F32), (HDIM, group)))[:, :1]
    bias[:group, :] = jnp.where(ids_down <= ids.astype(F32), 0.0, NEGATIVE)
    bias[group:, :] = jnp.zeros((group, group), F32) + jnp.where(has_before, 0.0, NEGATIVE)
    weight = jnp.zeros(ids.shape, F32)
    for index in range(steps_ref.shape[1]):
        weight = jnp.where(ids == index, steps_ref[0, index].astype(F32), weight)
    weight_row[...] = weight

    for a in range(4):
        incoming_local(a).wait()

    def forward(c):
        for a in (0, 1):
            for d in peers:
                incoming(a, c, d).wait_recv()

            @pl.when(has_after)
            def _():
                ahead(a, c).start()

    def one_block(head, block_index):
        cols = pl.ds(pl.multiple_of(head * HDIM, HDIM), HDIM)
        if query_block == group:
            rows = pl.ds(0, group)
        else:
            rows = pl.ds(pl.multiple_of(block_index * query_block, query_block), query_block)
        query = heads_query[rows, cols]
        grad = heads_grad[rows, cols]
        keys = key_joined[:, cols]
        scores = dot(keys, query, 1, 1) * (scale * math.log2(math.e)) + bias[:, rows]
        top = jnp.max(scores, axis=0, keepdims=True)
        raised = jnp.exp2(scores - top)
        inverse_total = 1.0 / jnp.sum(raised, axis=0, keepdims=True)
        grad_prob = dot(value_joined[:, cols], grad, 1, 1)
        delta = jnp.sum(raised * grad_prob, axis=0, keepdims=True) * inverse_total
        weighted = raised * (weight_row[:, rows] * inverse_total)
        sgrad = (weighted * (grad_prob - delta)).astype(BF16)
        weights = weighted.astype(BF16)
        dq_heads[rows, cols] = (dot(sgrad, keys, 0, 0) * scale).astype(BF16)
        return dot(sgrad, query, 1, 0) * scale, dot(weights, grad, 1, 0)

    def one_head(head):
        cols = pl.ds(pl.multiple_of(head * HDIM, HDIM), HDIM)
        if query_block == group:
            key_term, value_term = one_block(head, 0)
        else:
            zero = jnp.zeros((2 * group, HDIM), F32)

            def add(i, total):
                terms = one_block(head, i)
                return total[0] + terms[0], total[1] + terms[1]

            key_term, value_term = lax.fori_loop(0, group // query_block, add, (zero, zero))
        own_key[:, cols] = key_term[:group]
        own_value[:, cols] = value_term[:group]
        send_key[:, cols] = key_term[group:].astype(BF16)
        send_value[:, cols] = value_term[group:].astype(BF16)

    def compute(c):
        for a in (2, 3):
            for d in peers:
                incoming(a, c, d).wait_recv()

        @pl.when(has_before)
        def _():
            for a in (0, 1):
                ahead(a, c).wait_recv()

        def head_step(i, carry):
            one_head(c * per_chunk + i)
            return carry

        lax.fori_loop(0, per_chunk, head_step, 0)

        @pl.when(has_before)
        def _():
            for a in (0, 1):
                behind(a, c).start()

        for d in peers:
            outgoing(0, c, d).start()
        outgoing_local(0, c).start()

    def finish(c):
        cols = columns(c)

        @pl.when(has_after)
        def _():
            for a in (0, 1):
                behind(a, c).wait_recv()

        for a, own, back in ((1, own_key, back_key), (2, own_value, back_value)):
            results[a][:, cols] = (own[:, cols] + back[:, cols].astype(F32)).astype(BF16)
            for d in peers:
                outgoing(a, c, d).start()
            outgoing_local(a, c).start()

    forward(0)

    def chunk_step(c, carry):
        @pl.when(c + 1 < chunks)
        def _():
            forward(c + 1)

        @pl.when(c < chunks)
        def _():
            compute(c)

        @pl.when(c > 0)
        def _():
            finish(c - 1)

        return carry

    lax.fori_loop(0, chunks + 1, chunk_step, 0)

    def arrive(a):
        def wait(c, carry):
            for d in peers:
                outgoing(a, c, d).wait_recv()
            outgoing_local(a, c).wait()
            return carry

        lax.fori_loop(0, chunks, wait, 0)

    def norm_backward(raw_ref, row, inverse_ref, rows_ref, out_ref):
        gain_rows[...] = jnp.zeros_like(gain_rows)

        def block(i, carry):
            rows = pl.ds(pl.multiple_of(i * ROWS, ROWS), ROWS)
            inverse = inverse_ref[rows, :]
            normal = raw_ref[0, rows, :].astype(F32) * inverse
            upstream = rows_ref[rows, :].astype(F32)
            scaled = upstream * gain_full[row : row + 1, :]
            inner = jnp.sum(scaled * normal, axis=1, keepdims=True) * (1.0 / channels)
            out_ref[0, rows, :] = (inverse * (scaled - normal * inner)).astype(BF16)
            gain_rows[...] += upstream * normal
            return carry

        lax.fori_loop(0, tokens // ROWS, block, 0)
        gain_part[row : row + 1, :] = jnp.sum(gain_rows[...], axis=0, keepdims=True)

    arrive(0)
    norm_backward(query_ref, 0, q_inverse, dq_rows, query_out)
    arrive(1)
    norm_backward(key_ref, 1, k_inverse, dk_rows, key_out)

    def pair_copy(d):
        peer = lax.rem(f + d, n_fsdp)
        return remote(
            gain_part.at[:, pl.ds(pl.multiple_of(peer * part, HDIM), part)],
            pair_recv.at[d - 1], pair_s.at[d - 1], pair_r.at[d - 1], {"fsdp": peer},
        )

    for d in range(1, n_fsdp):
        pair_copy(d).start()
    arrive(2)
    value_out[0] = dv_rows[...]
    total = gain_part[:, pl.ds(pl.multiple_of(f * part, HDIM), part)]
    for d in range(1, n_fsdp):
        pair_copy(d).wait_recv()
        total = total + pair_recv[d - 1]
    tree_copies = []
    for b, (axis, device) in enumerate(tree):
        tree_send[b] = total
        copy = remote(
            tree_send.at[b], tree_recv.at[b], tree_s.at[b], tree_r.at[b], {axis: device}
        )
        copy.start()
        copy.wait_recv()
        total = tree_send[b] + tree_recv[b]
        tree_copies.append(copy)
    gain_out[...] = total

    for copy in tree_copies:
        copy.wait_send()
    for d in range(1, n_fsdp):
        gain_copy(d).wait_send()
        pair_copy(d).wait_send()

    def drain(c, carry):
        for d in peers:
            for a in range(4):
                incoming(a, c, d).wait_send()
            for a in range(3):
                outgoing(a, c, d).wait_send()

        @pl.when(has_after)
        def _():
            for a in (0, 1):
                ahead(a, c).wait_send()

        @pl.when(has_before)
        def _():
            for a in (0, 1):
                behind(a, c).wait_send()

        return carry

    lax.fori_loop(0, chunks, drain, 0)


def on_device(sizes, query_pre, key_pre, values, cotangent, gains, frame_span, denoise_steps):
    n_span, n_sp, n_fsdp = sizes
    _, tokens, channels = query_pre.shape
    group, width, part = tokens * n_sp, channels // n_sp, channels // n_fsdp
    heads = width // HDIM
    per_chunk = max(1, heads // 4)
    chunks = heads // per_chunk
    tree = max(1, (n_sp.bit_length() - 1) + (n_span.bit_length() - 1))
    vmem = pltpu.VMEM
    dma = pltpu.SemaphoreType.DMA
    scratch = [
        vmem((2, channels), F32),
        vmem((tokens, channels), BF16), vmem((tokens, channels), BF16),
        vmem((tokens, 1), F32), vmem((tokens, 1), F32),
        vmem((group, width), BF16), vmem((group, width), BF16),
        vmem((2 * group, width), BF16), vmem((2 * group, width), BF16),
        vmem((2 * group, group), F32), vmem((1, group), F32),
        vmem((group, width), F32), vmem((group, width), F32),
        vmem((group, width), BF16), vmem((group, width), BF16),
        vmem((group, width), BF16), vmem((group, width), BF16),
        vmem((group, width), BF16), vmem((group, width), BF16), vmem((group, width), BF16),
        vmem((tokens, channels), BF16), vmem((tokens, channels), BF16),
        vmem((tokens, channels), BF16),
        vmem((2, channels), F32), vmem((ROWS, channels), F32),
        vmem((max(1, n_fsdp - 1), 2, part), F32),
        vmem((tree, 2, part), F32), vmem((tree, 2, part), F32),
        dma((max(1, n_fsdp - 1),)), dma((max(1, n_fsdp - 1),)),
        dma((4, chunks, max(1, n_sp - 1))), dma((4, chunks, max(1, n_sp - 1))), dma((4,)),
        dma((2, chunks)), dma((2, chunks)), dma((2, chunks)), dma((2, chunks)),
        dma((3, chunks, max(1, n_sp - 1))), dma((3, chunks, max(1, n_sp - 1))),
        dma((3, chunks)),
        dma((max(1, n_fsdp - 1),)), dma((max(1, n_fsdp - 1),)), dma((tree,)), dma((tree,)),
    ]
    in_vmem = pl.BlockSpec(memory_space=pltpu.VMEM)
    pairs = heads * group * 2 * group
    return pl.pallas_call(
        functools.partial(kernel, (n_span, n_sp, n_fsdp, chunks, per_chunk)),
        out_shape=(
            jax.ShapeDtypeStruct(query_pre.shape, BF16),
            jax.ShapeDtypeStruct(query_pre.shape, BF16),
            jax.ShapeDtypeStruct(query_pre.shape, BF16),
            jax.ShapeDtypeStruct((2, part), F32),
        ),
        in_specs=[in_vmem] * 6 + [pl.BlockSpec(memory_space=pltpu.SMEM)],
        out_specs=[in_vmem] * 4,
        scratch_shapes=scratch,
        cost_estimate=pl.CostEstimate(
            flops=10 * pairs * HDIM, bytes_accessed=14 * tokens * channels, transcendentals=pairs
        ),
        compiler_params=pltpu.CompilerParams(
            collective_id=0, has_side_effects=True, vmem_limit_bytes=56 * 2**20
        ),
    )(query_pre, key_pre, values, cotangent, gains, frame_span, denoise_steps)


def solution(mesh):
    sizes = (mesh.shape["span"], mesh.shape["sp"], mesh.shape["fsdp"])
    rows = P("fsdp", ("span", "sp"), None)
    return jax.shard_map(
        functools.partial(on_device, sizes),
        mesh=mesh,
        in_specs=(rows, rows, rows, rows, P(None, "fsdp"), P("fsdp", "span"), P("fsdp", None)),
        out_specs=(rows, rows, rows, P(None, "fsdp")),
        check_vma=False,
    )
```

time: 340 us -> 118 us (0.35)
  the two profiles are of different devices: /device:TPU:0 before, /device:TPU:10 now
where the time goes in v1:
time: 118 us
  Pallas kernels  112 us (95%)
  local copies, waits for them, and re-layouts  5.04 us (4%)
    pallas_call x1, Pallas kernels, on_device(): pl.pallas_call(functools.partial(kernel, (n_span, n_sp, n_fsdp, chunks, p...  112 us
    unnamed x10, local copies, waits for them, and re-layouts  5.04 us

profile of v1, /device:TPU:10, one launch (start us, length us, event | category | flops | bytes accessed | tf_op | source)
XLA Modules:
  0.0 117.6 jit_solution(18088918760420174560)
XLA Ops:
  0.6 111.9 %shard_map.102 = (bf16[1,128,3072]{2,1,0:T(8,128)(2,1)}, bf16[1,128,3072]{2,1,0:T(8,128)(2,1)}, bf16[1,128,3072]{2,1,0:T(8,128)(2,1)}, f32[2,1536]{1,0:T(2,128)}) custom-call(bf16[1,128,3072]{2,1,0:T(8,128)(2,1)} %query_ref.1, bf16[1,128,3072]{2,1,0:T(8,128)(2,1)} %key_ref.1, bf16[1,128,3072]{2,1,0:T(8,128)(2,1)} %value_ref.1, ...), custom_call_target="tpu_custom_call" | custom-call | flops 2013265920 | bytes 5505024 | tf_op jit(solution)/shard_map/pallas_call | solution.py:443
  112.6 0.0 copy-start.1
  112.6 2.1 %copy.15 = bf16[1,128,3072]{2,1,0:T(8,128)(2,1)} copy(bf16[1,128,3072]{2,1,0:T(8,128)(2,1)} %get-tuple-element.8) | data formatting | bytes 1572864
  114.7 0.0 copy-done.1
  114.7 0.0 copy-start
  114.7 0.9 copy.16
  115.6 0.5 copy-done
  116.1 0.0 copy-start.2
  116.1 0.9 copy.17
  117.0 0.0 copy-done.2
  117.0 0.6 copy.18
Async XLA Ops:
  112.6 2.1 %copy-start.1 = (bf16[1,128,3072]{2,1,0:T(8,128)(2,1)S(1)}, bf16[1,128,3072]{2,1,0:T(8,128)(2,1)}, u32[]{:S(2)}) copy-start(bf16[1,128,3072]{2,1,0:T(8,128)(2,1)} %get-tuple-element.9) | copy-start | bytes 2359300
  114.7 1.4 %copy-start = (bf16[1,128,3072]{2,1,0:T(8,128)(2,1)S(1)}, bf16[1,128,3072]{2,1,0:T(8,128)(2,1)}, u32[]{:S(2)}) copy-start(bf16[1,128,3072]{2,1,0:T(8,128)(2,1)} %get-tuple-element.10) | copy-start | bytes 2359300
  116.1 0.9 copy-start.2

commit v2 on v1

--- a/solution.py
+++ b/solution.py
@@ -20,6 +20,15 @@
     return lax.dot_general(
         left, right, (((left_dim,), (right_dim,)), ((), ())), preferred_element_type=F32
     )
+
+
+def stages_of(devices):
+    stages, stride = [], 1
+    while devices > 1:
+        size = next((n for n in (4, 2, 3) if devices % n == 0), devices)
+        stages.append((stride, size))
+        stride, devices = stride * size, devices // size
+    return stages
 
 
 def kernel(
@@ -45,13 +54,17 @@
     after, before = lax.rem(g + 1, n_span), lax.rem(g + n_span - 1, n_span)
     has_before, has_after = g > 0, g < n_span - 1
 
-    def partner(index, step):
-        return index + step * (1 - 2 * lax.rem(index // step, 2))
-
-    sp_steps = [1 << b for b in range(n_sp.bit_length() - 1)]
-    span_steps = [1 << b for b in range(n_span.bit_length() - 1)]
-    tree = [("sp", partner(s, step)) for step in sp_steps]
-    tree += [("span", partner(g, step)) for step in span_steps]
+    place = g * n_sp + s
+
+    def digit(stage):
+        return lax.rem(lax.div(place, stage[0]), stage[1])
+
+    def tree_peer(stage, d):
+        mine = digit(stage)
+        other = place + (lax.rem(mine + d, stage[1]) - mine) * stage[0]
+        return {"span": lax.div(other, n_sp), "sp": lax.rem(other, n_sp)}
+
+    tree = stages_of(n_span * n_sp)
 
     barrier = pltpu.get_barrier_semaphore()
 
@@ -67,9 +80,10 @@
     for d in range(1, n_sp):
         greet({"sp": lax.rem(s + d, n_sp)})
         count += 1
-    for step in span_steps[1:]:
-        greet({"span": partner(g, step)})
-        count += 1
+    for stage in tree:
+        for d in range(1, stage[1]):
+            greet(tree_peer(stage, d))
+            count += 1
 
     @pl.when(has_before)
     def _():
@@ -153,10 +167,16 @@
     peers = range(1, n_sp)
     for d in range(1, n_fsdp):
         gain_copy(d).start()
-    for a in (1, 3):
-        for d in peers:
-            incoming(a, 0, d).start()
+    early = min(3, chunks)
+
+    def start_early(a):
+        for c in range(early):
+            for d in peers:
+                incoming(a, c, d).start()
         incoming_local(a).start()
+
+    start_early(1)
+    start_early(3)
     gain_full[:, pl.ds(pl.multiple_of(f * part, HDIM), part)] = gain_ref[...]
 
     @pl.when(g == 0)
@@ -186,13 +206,9 @@
         lax.fori_loop(0, tokens // ROWS, block, 0)
 
     norm(key_ref, 1, k_inverse, k_ready)
-    for d in peers:
-        incoming(0, 0, d).start()
-    incoming_local(0).start()
+    start_early(0)
     norm(query_ref, 0, q_inverse, q_ready)
-    for d in peers:
-        incoming(2, 0, d).start()
-    incoming_local(2).start()
+    start_early(2)
 
     def start_chunk(c, carry):
         for a in range(4):
@@ -200,7 +216,7 @@
                 incoming(a, c, d).start()
         return carry
 
-    lax.fori_loop(1, chunks, start_chunk, 0)
+    lax.fori_loop(early, chunks, start_chunk, 0)
 
     ids = span_ref[...]
     ids_down = jnp.transpose(jnp.broadcast_to(ids.astype(F32), (HDIM, group)))[:, :1]
@@ -300,24 +316,26 @@
                 outgoing(a, c, d).start()
             outgoing_local(a, c).start()
 
-    forward(0)
+    lead = min(2, chunks)
+    for c in range(lead):
+        forward(c)
 
     def chunk_step(c, carry):
-        @pl.when(c + 1 < chunks)
-        def _():
-            forward(c + 1)
+        @pl.when(c + lead < chunks)
+        def _():
+            forward(c + lead)
 
         @pl.when(c < chunks)
         def _():
             compute(c)
 
-        @pl.when(c > 0)
-        def _():
-            finish(c - 1)
+        @pl.when(c >= lead)
+        def _():
+            finish(c - lead)
 
         return carry
 
-    lax.fori_loop(0, chunks + 1, chunk_step, 0)
+    lax.fori_loop(0, chunks + lead, chunk_step, 0)
 
     def arrive(a):
         def wait(c, carry):
@@ -366,15 +384,24 @@
         pair_copy(d).wait_recv()
         total = total + pair_recv[d - 1]
     tree_copies = []
-    for b, (axis, device) in enumerate(tree):
+    for b, stage in enumerate(tree):
         tree_send[b] = total
-        copy = remote(
-            tree_send.at[b], tree_recv.at[b], tree_s.at[b], tree_r.at[b], {axis: device}
-        )
-        copy.start()
-        copy.wait_recv()
-        total = tree_send[b] + tree_recv[b]
-        tree_copies.append(copy)
+        copies = [
+            remote(
+                tree_send.at[b], tree_recv.at[b, digit(stage)],
+                tree_s.at[b, d - 1], tree_r.at[b, d - 1], tree_peer(stage, d),
+            )
+            for d in range(1, stage[1])
+        ]
+        for copy in copies:
+            copy.start()
+        tree_recv[b, digit(stage)] = total
+        for copy in copies:
+            copy.wait_recv()
+        total = tree_recv[b, 0]
+        for index in range(1, stage[1]):
+            total = total + tree_recv[b, index]
+        tree_copies += copies
     gain_out[...] = total
 
     for copy in tree_copies:
@@ -410,9 +437,11 @@
     _, tokens, channels = query_pre.shape
     group, width, part = tokens * n_sp, channels // n_sp, channels // n_fsdp
     heads = width // HDIM
-    per_chunk = max(1, heads // 4)
+    per_chunk = 1
     chunks = heads // per_chunk
-    tree = max(1, (n_sp.bit_length() - 1) + (n_span.bit_length() - 1))
+    stages = stages_of(n_span * n_sp)
+    tree = max(1, len(stages))
+    most = max([size for _, size in stages] + [2])
     vmem = pltpu.VMEM
     dma = pltpu.SemaphoreType.DMA
     scratch = [
@@ -430,13 +459,14 @@
         vmem((tokens, channels), BF16),
         vmem((2, channels), F32), vmem((ROWS, channels), F32),
         vmem((max(1, n_fsdp - 1), 2, part), F32),
-        vmem((tree, 2, part), F32), vmem((tree, 2, part), F32),
+        vmem((tree, 2, part), F32), vmem((tree, most, 2, part), F32),
         dma((max(1, n_fsdp - 1),)), dma((max(1, n_fsdp - 1),)),
         dma((4, chunks, max(1, n_sp - 1))), dma((4, chunks, max(1, n_sp - 1))), dma((4,)),
         dma((2, chunks)), dma((2, chunks)), dma((2, chunks)), dma((2, chunks)),
         dma((3, chunks, max(1, n_sp - 1))), dma((3, chunks, max(1, n_sp - 1))),
         dma((3, chunks)),
-        dma((max(1, n_fsdp - 1),)), dma((max(1, n_fsdp - 1),)), dma((tree,)), dma((tree,)),
+        dma((max(1, n_fsdp - 1),)), dma((max(1, n_fsdp - 1),)), dma((tree, most - 1)),
+        dma((tree, most - 1)),
     ]
     in_vmem = pl.BlockSpec(memory_space=pltpu.VMEM)
     pairs = heads * group * 2 * group

time: 118 us -> 111 us (0.941)
  the two profiles are of different devices: /device:TPU:10 before, /device:TPU:0 now
where the time goes in v2:
time: 111 us
  Pallas kernels  105 us (95%)
  local copies, waits for them, and re-layouts  5.04 us (5%)
    pallas_call x1, Pallas kernels, on_device(): pl.pallas_call(functools.partial(kernel, (n_span, n_sp, n_fsdp, chunks, p...  105 us
    unnamed x10, local copies, waits for them, and re-layouts  5.04 us

profile of v2, /device:TPU:0, one launch (start us, length us, event | category | flops | bytes accessed | tf_op | source)
XLA Modules:
  0.0 110.7 jit_solution(16536533468023490097)
XLA Ops:
  0.6 105.1 %shard_map.102 = (bf16[1,128,3072]{2,1,0:T(8,128)(2,1)}, bf16[1,128,3072]{2,1,0:T(8,128)(2,1)}, bf16[1,128,3072]{2,1,0:T(8,128)(2,1)}, f32[2,1536]{1,0:T(2,128)}) custom-call(bf16[1,128,3072]{2,1,0:T(8,128)(2,1)} %query_ref.1, bf16[1,128,3072]{2,1,0:T(8,128)(2,1)} %key_ref.1, bf16[1,128,3072]{2,1,0:T(8,128)(2,1)} %value_ref.1, ...), custom_call_target="tpu_custom_call" | custom-call | flops 2013265920 | bytes 5505024 | tf_op jit(solution)/shard_map/pallas_call | solution.py:473
  105.7 0.0 copy-start.1
  105.7 2.1 %copy.15 = bf16[1,128,3072]{2,1,0:T(8,128)(2,1)} copy(bf16[1,128,3072]{2,1,0:T(8,128)(2,1)} %get-tuple-element.8) | data formatting | bytes 1572864
  107.8 0.0 copy-done.1
  107.8 0.0 copy-start
  107.8 0.9 copy.16
  108.7 0.5 copy-done
  109.3 0.0 copy-start.2
  109.3 0.9 copy.17
  110.1 0.0 copy-done.2
  110.1 0.6 copy.18
Async XLA Ops:
  105.7 2.1 %copy-start.1 = (bf16[1,128,3072]{2,1,0:T(8,128)(2,1)S(1)}, bf16[1,128,3072]{2,1,0:T(8,128)(2,1)}, u32[]{:S(2)}) copy-start(bf16[1,128,3072]{2,1,0:T(8,128)(2,1)} %get-tuple-element.9) | copy-start | bytes 2359300
  107.8 1.4 %copy-start = (bf16[1,128,3072]{2,1,0:T(8,128)(2,1)S(1)}, bf16[1,128,3072]{2,1,0:T(8,128)(2,1)}, u32[]{:S(2)}) copy-start(bf16[1,128,3072]{2,1,0:T(8,128)(2,1)} %get-tuple-element.10) | copy-start | bytes 2359300
  109.3 0.9 copy-start.2

commit v3 on v2

--- a/solution.py
+++ b/solution.py
@@ -316,7 +316,8 @@
                 outgoing(a, c, d).start()
             outgoing_local(a, c).start()
 
-    lead = min(2, chunks)
+    lead = min(3, chunks)
+    lag = min(3, chunks)
     for c in range(lead):
         forward(c)
 
@@ -329,13 +330,13 @@
         def _():
             compute(c)
 
-        @pl.when(c >= lead)
-        def _():
-            finish(c - lead)
+        @pl.when(c >= lag)
+        def _():
+            finish(c - lag)
 
         return carry
 
-    lax.fori_loop(0, chunks + lead, chunk_step, 0)
+    lax.fori_loop(0, chunks + lag, chunk_step, 0)
 
     def arrive(a):
         def wait(c, carry):

time: 111 us -> 108 us (0.973)
  Pallas kernels: 105 us -> 102 us
    pallas_call x1, Pallas kernels: 105 us -> 102 us  [on_device(): pl.pallas_call(functools.partial(kernel, (n_span, n_sp, n_fsdp, chunks, p...]
where the time goes in v3:
time: 108 us
  Pallas kernels  102 us (94%)
  local copies, waits for them, and re-layouts  5.04 us (5%)
    pallas_call x1, Pallas kernels, on_device(): pl.pallas_call(functools.partial(kernel, (n_span, n_sp, n_fsdp, chunks, p...  102 us
    unnamed x10, local copies, waits for them, and re-layouts  5.04 us

profile of v3, /device:TPU:0, one launch (start us, length us, event | category | flops | bytes accessed | tf_op | source)
XLA Modules:
  0.0 108.0 jit_solution(13043502716746561069)
XLA Ops:
  0.6 102.3 %shard_map.102 = (bf16[1,128,3072]{2,1,0:T(8,128)(2,1)}, bf16[1,128,3072]{2,1,0:T(8,128)(2,1)}, bf16[1,128,3072]{2,1,0:T(8,128)(2,1)}, f32[2,1536]{1,0:T(2,128)}) custom-call(bf16[1,128,3072]{2,1,0:T(8,128)(2,1)} %query_ref.1, bf16[1,128,3072]{2,1,0:T(8,128)(2,1)} %key_ref.1, bf16[1,128,3072]{2,1,0:T(8,128)(2,1)} %value_ref.1, ...), custom_call_target="tpu_custom_call" | custom-call | flops 2013265920 | bytes 5505024 | tf_op jit(solution)/shard_map/pallas_call | solution.py:474
  102.9 0.0 copy-start.1
  102.9 2.1 %copy.15 = bf16[1,128,3072]{2,1,0:T(8,128)(2,1)} copy(bf16[1,128,3072]{2,1,0:T(8,128)(2,1)} %get-tuple-element.8) | data formatting | bytes 1572864
  105.0 0.0 copy-done.1
  105.0 0.0 copy-start
  105.1 0.9 copy.16
  105.9 0.5 copy-done
  106.5 0.0 copy-start.2
  106.5 0.9 copy.17
  107.3 0.0 copy-done.2
  107.4 0.6 copy.18
Async XLA Ops:
  102.9 2.1 %copy-start.1 = (bf16[1,128,3072]{2,1,0:T(8,128)(2,1)S(1)}, bf16[1,128,3072]{2,1,0:T(8,128)(2,1)}, u32[]{:S(2)}) copy-start(bf16[1,128,3072]{2,1,0:T(8,128)(2,1)} %get-tuple-element.9) | copy-start | bytes 2359300
  105.0 1.4 %copy-start = (bf16[1,128,3072]{2,1,0:T(8,128)(2,1)S(1)}, bf16[1,128,3072]{2,1,0:T(8,128)(2,1)}, u32[]{:S(2)}) copy-start(bf16[1,128,3072]{2,1,0:T(8,128)(2,1)} %get-tuple-element.10) | copy-start | bytes 2359300
  106.5 0.9 copy-start.2

commit v4 on v3

--- a/solution.py
+++ b/solution.py
@@ -316,8 +316,8 @@
                 outgoing(a, c, d).start()
             outgoing_local(a, c).start()
 
-    lead = min(3, chunks)
-    lag = min(3, chunks)
+    lead = min(4, chunks)
+    lag = min(4, chunks)
     for c in range(lead):
         forward(c)
 

time: 108 us -> 109 us (level)
  Pallas kernels: 102 us -> 104 us
    pallas_call x1, Pallas kernels: 102 us -> 104 us  [on_device(): pl.pallas_call(functools.partial(kernel, (n_span, n_sp, n_fsdp, chunks, p...]
where the time goes in v4:
time: 109 us
  Pallas kernels  104 us (95%)
  local copies, waits for them, and re-layouts  5.04 us (5%)
    pallas_call x1, Pallas kernels, on_device(): pl.pallas_call(functools.partial(kernel, (n_span, n_sp, n_fsdp, chunks, p...  104 us
    unnamed x10, local copies, waits for them, and re-layouts  5.04 us

profile of v4, /device:TPU:0, one launch (start us, length us, event | category | flops | bytes accessed | tf_op | source)
XLA Modules:
  0.0 109.2 jit_solution(6018108623517998222)
XLA Ops:
  0.6 103.5 %shard_map.102 = (bf16[1,128,3072]{2,1,0:T(8,128)(2,1)}, bf16[1,128,3072]{2,1,0:T(8,128)(2,1)}, bf16[1,128,3072]{2,1,0:T(8,128)(2,1)}, f32[2,1536]{1,0:T(2,128)}) custom-call(bf16[1,128,3072]{2,1,0:T(8,128)(2,1)} %query_ref.1, bf16[1,128,3072]{2,1,0:T(8,128)(2,1)} %key_ref.1, bf16[1,128,3072]{2,1,0:T(8,128)(2,1)} %value_ref.1, ...), custom_call_target="tpu_custom_call" | custom-call | flops 2013265920 | bytes 5505024 | tf_op jit(solution)/shard_map/pallas_call | solution.py:474
  104.2 0.0 copy-start.1
  104.2 2.1 %copy.15 = bf16[1,128,3072]{2,1,0:T(8,128)(2,1)} copy(bf16[1,128,3072]{2,1,0:T(8,128)(2,1)} %get-tuple-element.8) | data formatting | bytes 1572864
  106.3 0.0 copy-done.1
  106.3 0.0 copy-start
  106.3 0.9 copy.16
  107.2 0.5 copy-done
  107.7 0.0 copy-start.2
  107.7 0.9 copy.17
  108.6 0.0 copy-done.2
  108.6 0.6 copy.18
Async XLA Ops:
  104.2 2.1 %copy-start.1 = (bf16[1,128,3072]{2,1,0:T(8,128)(2,1)S(1)}, bf16[1,128,3072]{2,1,0:T(8,128)(2,1)}, u32[]{:S(2)}) copy-start(bf16[1,128,3072]{2,1,0:T(8,128)(2,1)} %get-tuple-element.9) | copy-start | bytes 2359300
  106.3 1.4 %copy-start = (bf16[1,128,3072]{2,1,0:T(8,128)(2,1)S(1)}, bf16[1,128,3072]{2,1,0:T(8,128)(2,1)}, u32[]{:S(2)}) copy-start(bf16[1,128,3072]{2,1,0:T(8,128)(2,1)} %get-tuple-element.10) | copy-start | bytes 2359300
  107.7 0.9 copy-start.2
